TPU v7x, 768 devices: a whole 4x8x12 slice. The times are simulated.
768 devices in a mesh: grp: 8 (over y), peer: 96 (over z, x, core).
Axes of the slice: x: 4, y: 8, z: 12, core: 2. Of those that a mesh axis runs over, the one named last changes fastest.
Arguments:
- state: float32 [393216, 288], P(('grp', 'peer')), may hold values from -6 to 6
- cost: int32 [393216], P(('grp', 'peer')), may hold values from 0 to 48, as said below
- links: int32 [768, 64], P(('grp', 'peer')), may hold values from 0 to 63, each once within a row
- dyn_weight: bfloat16 [288, 288], replicated, may hold values from -0.375 to 0.375
- rad_weight: bfloat16 [288, 288], replicated, may hold values from -0.375 to 0.375
- cloud_weight: bfloat16 [288, 288], replicated, may hold values from -0.375 to 0.375
Outputs:
- state_next: float32 [393216, 288], P(('grp', 'peer'))
Inputs may be any that keep to these rules, and one draw needn't show every extreme that they name: A column is cloudy where its cost is above 0. A block of 512 consecutive columns holds at most 192 cloudy columns; every aligned group of 96 such blocks holds exactly 4608 cloudy columns, and one block of each group exactly 192. `links`: each row is a permutation of 0 to 63.
All inputs are finite; a program needn't handle non-finite values.
Results may differ from a plain program's by a relative error of at most 0.0039.
Values may be sent and summed in bfloat16 or wider, within the bound.
A program may use at most 32 MiB of HBM per device.

v0:
```python
import jax
import jax.numpy as jnp
from jax import lax
from jax.sharding import PartitionSpec as P

LEV = 48
SPAN = 48
EDGE = 64
MICRO = 24
SUBSTEPS = 3


def carried_in(array, axis, combine, identity):
    length, mine = (lax.axis_size(axis), lax.axis_index(axis))
    everything = lax.all_gather(array, axis)
    start = jnp.broadcast_to(jnp.asarray(identity, array.dtype), array.shape)

    def turn(k, before):
        reached = k < mine
        new = combine(before, everything[k])
        return jnp.where(reached, new, before)

    return lax.fori_loop(0, length, turn, start)


def from_behind(array, axis, by):
    length = lax.axis_size(axis)
    return lax.ppermute(array, axis, [(i, (i + by) % length) for i in range(length)])


def cloud_physics(rows_in, cloud_depth, cloud_weight):
    width = rows_in.shape[1]
    level_index = jnp.arange(width, dtype=jnp.int32) % LEV
    level_mask = (level_index[None, :] >= (LEV - cloud_depth)[:, None]).astype(jnp.float32)
    initial = rows_in.astype(jnp.float32)

    def micro_turn(count, iterate):
        forcing = jnp.tanh(
            jnp.dot(iterate.astype(jnp.bfloat16), cloud_weight, preferred_element_type=jnp.float32)
        )
        return iterate + 0.1 * level_mask * forcing

    finished = lax.fori_loop(0, MICRO, micro_turn, initial)
    return (finished - initial).astype(jnp.bfloat16)


def add_counts(earlier, later):
    return earlier + later


def dynamics(rows, dyn_weight):
    return rows + 0.2 * jnp.dot(
        rows.astype(jnp.bfloat16), dyn_weight, preferred_element_type=jnp.float32
    )


def per_device(state, cost, links, dyn_weight, rad_weight, cloud_weight):
    column_count = state.shape[0]
    width = state.shape[1]
    initial = state.astype(jnp.bfloat16)
    heating = jnp.dot(initial, rad_weight, preferred_element_type=jnp.float32)
    cloudy = cost > 0
    cloud_index = jnp.maximum(jnp.cumsum(cloudy.astype(jnp.int32)) - 1, 0)
    cloud_total = jnp.sum(cloudy.astype(jnp.int32))
    listing = jnp.nonzero(cloudy, size=4 * SPAN, fill_value=0)[0].astype(jnp.int32)
    peer_count = lax.axis_size("peer")
    slot_count = (4 * SPAN + peer_count - 1) // peer_count
    before = carried_in(cloud_total, "peer", add_counts, jnp.int32(0))
    target = jnp.arange(peer_count, dtype=jnp.int32)[:, None]
    slot_index = jnp.arange(slot_count, dtype=jnp.int32)[None, :]
    list_index = slot_index * peer_count + (target - before) % peer_count
    is_live = list_index < cloud_total
    picked = listing[jnp.minimum(list_index, 4 * SPAN - 1)]
    packed = jnp.where(is_live[:, :, None], initial[picked], jnp.zeros((), jnp.bfloat16))
    depth_sent = jnp.where(is_live, cost[picked], 0).astype(jnp.bfloat16)
    received, depth_got = (
        lax.all_to_all(packed, "peer", split_axis=0, concat_axis=0, tiled=True),
        lax.all_to_all(depth_sent, "peer", split_axis=0, concat_axis=0, tiled=True),
    )
    flat_rows = received.reshape(peer_count * slot_count, width)
    flat_depth = depth_got.reshape(peer_count * slot_count).astype(jnp.int32)
    held_rows = jnp.nonzero(flat_depth > 0, size=SPAN, fill_value=0)[0].astype(jnp.int32)
    change = cloud_physics(flat_rows[held_rows], flat_depth[held_rows], cloud_weight)
    answer = jnp.zeros((peer_count * slot_count, width), jnp.bfloat16).at[held_rows].set(change)
    returned = lax.all_to_all(
        answer.reshape(peer_count, slot_count, width),
        "peer",
        split_axis=0,
        concat_axis=0,
        tiled=True,
    )
    flat_back = returned.reshape(peer_count * slot_count, width)
    location = (before + cloud_index) % peer_count * slot_count + cloud_index // peer_count
    location = jnp.minimum(location, peer_count * slot_count - 1)
    cloud_term = jnp.where(cloudy[:, None], flat_back[location].astype(jnp.float32), 0.0)
    link_row = links[0]
    column_state = state
    for substep in range(SUBSTEPS):
        column_state = dynamics(column_state, dyn_weight)
        left_rim = column_state[:EDGE]
        right_rim = column_state[column_count - EDGE :]
        prev_right = from_behind(right_rim.astype(jnp.bfloat16), ("grp", "peer"), 1).astype(
            right_rim.dtype
        )
        new_left = 0.5 * (left_rim + prev_right[link_row])
        back_local = jnp.zeros_like(right_rim).at[link_row].set(new_left)
        new_right = from_behind(back_local.astype(jnp.bfloat16), ("grp", "peer"), -1).astype(
            back_local.dtype
        )
        column_state = jnp.concatenate(
            [new_left, column_state[EDGE : column_count - EDGE], new_right], axis=0
        )
    return column_state + 0.25 * heating + cloud_term


def solution(mesh):
    return jax.shard_map(
        per_device,
        mesh=mesh,
        in_specs=(
            P(("grp", "peer"), None),
            P(("grp", "peer")),
            P(("grp", "peer"), None),
            P(),
            P(),
            P(),
        ),
        out_specs=P(("grp", "peer"), None),
        check_vma=False,
    )
```

profile of v0, /device:TPU:56, one launch (start us, length us, event | category | flops | bytes accessed | tf_op | source)
XLA Modules:
  0.0 440.0 jit_solution(17849771904704393409)
XLA Ops:
  0.0 1.4 copy.50
  1.8 1.9 collective-permute-start
  3.8 0.7 copy-done.1
  5.7 1.3 dynamic-slice
  7.0 1.4 dynamic-update-slice
  8.4 199.7 %all-reduce.2 = s32[96]{0:T(128)S(1)} all-reduce(s32[96]{0:T(128)S(1)} %dynamic-update-slice), channel_id=1, replica_groups=mesh['grp'=8,'peer'=96] {'peer'}, use_global_device_ids=true, to_apply=%add.2 | all-reduce | flops 96 | bytes 768
  208.1 126.1 %while.24 = (s32[]{:T(128)}, s32[]{:T(128)}, s32[]{:T(128)}, s32[96]{0:T(128)S(1)}, s32[]{:T(128)}) while((s32[]{:T(128)}, s32[]{:T(128)}, s32[]{:T(128)}, s32[96]{0:T(128)S(1)}, s32[]{:T(128)}) %tuple.46), condition=%wide.region_5.6_spmd, body=%wide.region_4.5_spmd.sunk | while | flops 5 | bytes 115 | solution.py:23
  209.4 0.7 dynamic_slice.8
  210.7 0.7 dynamic_slice.8
  212.0 0.7 dynamic_slice.8
  213.4 0.7 dynamic_slice.8
  214.7 0.7 dynamic_slice.8
  216.0 0.7 dynamic_slice.8
  217.3 0.7 dynamic_slice.8
  218.6 0.7 dynamic_slice.8
  219.9 0.7 dynamic_slice.8
  221.2 0.7 dynamic_slice.8
  222.6 0.7 dynamic_slice.8
  223.9 0.7 dynamic_slice.8
  225.2 0.7 dynamic_slice.8
  226.5 0.7 dynamic_slice.8
  227.8 0.7 dynamic_slice.8
  229.1 0.7 dynamic_slice.8
  230.4 0.7 dynamic_slice.8
  231.8 0.7 dynamic_slice.8
  334.3 4.1 scatter_custom_fusion.3
  339.0 0.7 compare_select_fusion.9
  339.9 1.6 gather_fusion.3
  341.9 1.6 gather_fusion.4
  343.7 0.7 fusion.32
  344.4 0.7 copy.55
  345.2 6.3 %all-to-all-start = ((bf16[96,1,2]{2,1,0:T(2,128)(2,1)}), bf16[96,1,2]{2,1,0:T(2,128)(2,1)S(1)}, u32[]{:S(2)}, u32[]{:S(2)}) async-start(bf16[96,1,2]{2,1,0:T(2,128)(2,1)} %copy.55), calls=%async_computation | async-start | bytes 98304 | tf_op jit(solution)/shard_map/all_to_all | solution.py:78
  351.5 0.7 add_compare_fusion
  352.3 1.0 gather_fusion.5
  353.5 0.9 broadcast_select_fusion
  354.4 9.0 %all-to-all-done = bf16[96,1,2]{2,1,0:T(2,128)(2,1)S(1)} async-done(((bf16[96,1,2]{2,1,0:T(2,128)(2,1)}), bf16[96,1,2]{2,1,0:T(2,128)(2,1)S(1)}, u32[]{:S(2)}, u32[]{:S(2)}) %all-to-all-start) | async-done | bytes 416 | tf_op jit(solution)/shard_map/all_to_all | solution.py:78
  363.4 5.9 %all-to-all-start.1 = ((bf16[96,2,288]{2,1,0:T(2,128)(2,1)}), bf16[96,2,288]{2,1,0:T(2,128)(2,1)S(1)}, u32[]{:S(2)}, u32[]{:S(2)}) async-start(bf16[96,2,288]{2,1,0:T(2,128)(2,1)} %broadcast_select_fusion), calls=%async_computation.1 | async-start | bytes 294912 | tf_op jit(solution)/shard_map/all_to_all | solution.py:77
  370.4 0.7 gather_fusion
  371.1 0.8 scatter_custom_fusion
  371.9 7.6 %collective-permute-start.1 = (bf16[64,288]{1,0:T(8,128)(2,1)S(1)}, bf16[64,288]{1,0:T(8,128)(2,1)S(1)}, u32[]{:S(2)}, u32[]{:S(2)}) collective-permute-start(bf16[64,288]{1,0:T(8,128)(2,1)S(1)} %convert_element_type.91), channel_id=1, source_target_pairs={{0,767},{1,0},{2,1},{3,2},{4,3},{5,4},{6,5},{7,6},{8,7},{9,8},{10,... | collective-permute-start | bytes 110600 | tf_op jit(solution)/shard_map/ppermute | solution.py:28
  379.6 0.7 fusion.33
  380.3 1.9 scatter_custom_fusion.4
  382.8 1.9 collective-permute-start.2
  384.7 0.8 fusion.25
  385.5 6.9 %collective-permute-done.2 = bf16[64,288]{1,0:T(8,128)(2,1)S(1)} collective-permute-done((bf16[64,288]{1,0:T(8,128)(2,1)S(1)}, bf16[64,288]{1,0:T(8,128)(2,1)S(1)}, u32[]{:S(2)}, u32[]{:S(2)}) %collective-permute-start.2) | collective-permute-done | bytes 36896 | tf_op jit(solution)/shard_map/ppermute | solution.py:28
  392.4 0.7 gather_fusion.1
  393.1 0.8 scatter_custom_fusion.1
  393.9 1.9 collective-permute-start.3
  395.9 0.8 gather_fusion.7
  396.7 0.9 collective-permute-done.3
  398.0 2.1 collective-permute-start.4
  400.1 7.5 %collective-permute-done.4 = bf16[64,288]{1,0:T(8,128)(2,1)S(1)} collective-permute-done((bf16[64,288]{1,0:T(8,128)(2,1)S(1)}, bf16[64,288]{1,0:T(8,128)(2,1)S(1)}, u32[]{:S(2)}, u32[]{:S(2)}) %collective-permute-start.4) | collective-permute-done | bytes 36896 | tf_op jit(solution)/shard_map/ppermute | solution.py:28
  407.7 0.7 gather_fusion.2
  408.5 0.7 gather_fusion.6
  409.4 4.9 %while.25 = (s32[]{:T(128)}, f32[48,288]{1,0:T(8,128)S(1)}, bf16[288,288]{1,0:T(8,128)(2,1)S(1)}, s32[48]{0:T(128)S(1)}, s32[288]{0:T(512)S(1)}, /*index=5*/s32[]{:T(128)}) while((s32[]{:T(128)}, f32[48,288]{1,0:T(8,128)S(1)}, bf16[288,288]{1,0:T(8,128)(2,1)S(1)}, s32[48]{0:T(128)S(1)}, s32[288]{0:T(512)S(1)}, ...), condition=%wide.region_17.18_spmd.clone, body=%wide.region_16.17_spmd.clone.sunk | while | flops 8031746 | bytes 388485 | solution.py:43
  414.3 0.8 scatter_custom_fusion.5
  415.1 0.7 reshape.429
  415.9 5.9 %all-to-all-start.2 = ((bf16[96,2,288]{2,1,0:T(2,128)(2,1)}), bf16[96,2,288]{2,1,0:T(2,128)(2,1)S(1)}, u32[]{:S(2)}, u32[]{:S(2)}) async-start(bf16[96,2,288]{2,1,0:T(2,128)(2,1)} %reshape.429), calls=%async_computation.2 | async-start | bytes 294912 | tf_op jit(solution)/shard_map/all_to_all | solution.py:85
  421.8 0.8 scatter_custom_fusion.2
  422.7 7.6 %collective-permute-start.5 = (bf16[64,288]{1,0:T(8,128)(2,1)S(1)}, bf16[64,288]{1,0:T(8,128)(2,1)S(1)}, u32[]{:S(2)}, u32[]{:S(2)}) collective-permute-start(bf16[64,288]{1,0:T(8,128)(2,1)S(1)} %convert_element_type.99), channel_id=1, source_target_pairs={{0,767},{1,0},{2,1},{3,2},{4,3},{5,4},{6,5},{7,6},{8,7},{9,8},{10,... | collective-permute-start | bytes 110600 | tf_op jit(solution)/shard_map/ppermute | solution.py:28
  430.4 1.7 collective-permute-done.5
  432.1 4.4 all-to-all-done.2
  436.6 1.9 gather_fusion.8
  439.0 1.1 copy.60
  (217 shorter events, 61.2 us)
Async XLA Ops:
  0.0 1.4 copy-start
  1.8 368.6 %collective-permute-start = (bf16[64,288]{1,0:T(8,128)(2,1)S(1)}, bf16[64,288]{1,0:T(8,128)(2,1)S(1)}, u32[]{:S(2)}, u32[]{:S(2)}) collective-permute-start(bf16[64,288]{1,0:T(8,128)(2,1)S(1)} %slice.116), channel_id=1, source_target_pairs={{0,1},{1,2},{2,3},{3,4},{4,5},{5,6},{6,7},{7,8},{8,9},{9,10},{10,1... | collective-permute-start | bytes 110600 | tf_op jit(solution)/shard_map/ppermute | solution.py:28
  3.7 0.7 copy-start.1
  345.2 18.2 %all-to-all-start = ((bf16[96,1,2]{2,1,0:T(2,128)(2,1)}), bf16[96,1,2]{2,1,0:T(2,128)(2,1)S(1)}, u32[]{:S(2)}, u32[]{:S(2)}) async-start(bf16[96,1,2]{2,1,0:T(2,128)(2,1)} %copy.55), calls=%async_computation | async-start | bytes 98304 | tf_op jit(solution)/shard_map/all_to_all | solution.py:78
  351.5 0.7 copy-start.5
  363.4 45.0 %all-to-all-start.1 = ((bf16[96,2,288]{2,1,0:T(2,128)(2,1)}), bf16[96,2,288]{2,1,0:T(2,128)(2,1)S(1)}, u32[]{:S(2)}, u32[]{:S(2)}) async-start(bf16[96,2,288]{2,1,0:T(2,128)(2,1)} %broadcast_select_fusion), calls=%async_computation.1 | async-start | bytes 294912 | tf_op jit(solution)/shard_map/all_to_all | solution.py:77
  371.9 10.4 %collective-permute-start.1 = (bf16[64,288]{1,0:T(8,128)(2,1)S(1)}, bf16[64,288]{1,0:T(8,128)(2,1)S(1)}, u32[]{:S(2)}, u32[]{:S(2)}) collective-permute-start(bf16[64,288]{1,0:T(8,128)(2,1)S(1)} %convert_element_type.91), channel_id=1, source_target_pairs={{0,767},{1,0},{2,1},{3,2},{4,3},{5,4},{6,5},{7,6},{8,7},{9,8},{10,... | collective-permute-start | bytes 110600 | tf_op jit(solution)/shard_map/ppermute | solution.py:28
  382.8 9.6 %collective-permute-start.2 = (bf16[64,288]{1,0:T(8,128)(2,1)S(1)}, bf16[64,288]{1,0:T(8,128)(2,1)S(1)}, u32[]{:S(2)}, u32[]{:S(2)}) collective-permute-start(bf16[64,288]{1,0:T(8,128)(2,1)S(1)} %slice.115), channel_id=1, source_target_pairs={{0,1},{1,2},{2,3},{3,4},{4,5},{5,6},{6,7},{7,8},{8,9},{9,10},{10,1... | collective-permute-start | bytes 110600 | tf_op jit(solution)/shard_map/ppermute | solution.py:28
  393.9 3.7 collective-permute-start.3
  398.0 32.4 %copy-start.3 = (f32[512,288]{1,0:T(8,128)}, f32[512,288]{1,0:T(8,128)S(1)}, u32[]{:S(2)}) copy-start(f32[512,288]{1,0:T(8,128)S(1)} %fusion.5) | copy-start | bytes 1769476
  398.0 9.7 %collective-permute-start.4 = (bf16[64,288]{1,0:T(8,128)(2,1)S(1)}, bf16[64,288]{1,0:T(8,128)(2,1)S(1)}, u32[]{:S(2)}, u32[]{:S(2)}) collective-permute-start(bf16[64,288]{1,0:T(8,128)(2,1)S(1)} %slice.114), channel_id=1, source_target_pairs={{0,1},{1,2},{2,3},{3,4},{4,5},{5,6},{6,7},{7,8},{8,9},{9,10},{10,1... | collective-permute-start | bytes 110600 | tf_op jit(solution)/shard_map/ppermute | solution.py:28
  408.5 0.9 copy-start.2
  415.9 20.6 %all-to-all-start.2 = ((bf16[96,2,288]{2,1,0:T(2,128)(2,1)}), bf16[96,2,288]{2,1,0:T(2,128)(2,1)S(1)}, u32[]{:S(2)}, u32[]{:S(2)}) async-start(bf16[96,2,288]{2,1,0:T(2,128)(2,1)} %reshape.429), calls=%async_computation.2 | async-start | bytes 294912 | tf_op jit(solution)/shard_map/all_to_all | solution.py:85
  422.7 9.4 %collective-permute-start.5 = (bf16[64,288]{1,0:T(8,128)(2,1)S(1)}, bf16[64,288]{1,0:T(8,128)(2,1)S(1)}, u32[]{:S(2)}, u32[]{:S(2)}) collective-permute-start(bf16[64,288]{1,0:T(8,128)(2,1)S(1)} %convert_element_type.99), channel_id=1, source_target_pairs={{0,767},{1,0},{2,1},{3,2},{4,3},{5,4},{6,5},{7,6},{8,7},{9,8},{10,... | collective-permute-start | bytes 110600 | tf_op jit(solution)/shard_map/ppermute | solution.py:28
  436.6 2.0 slice-start
  436.6 2.0 copy-start.4
where the time goes:
time: 447 us; the launch traced here: 440 us
  blocking collectives  200 us (45%)
  local copies, waits for them, and re-layouts  84.4 us (19%)
  loops' own time  64.5 us (14%)
  starting transfers between devices  41.3 us (9%)
  waiting for transfers between devices  30.3 us (7%)
  other arithmetic  13.7 us (3%)
  matrix products  5.55 us (1%)
    unnamed x1, blocking collectives  200 us
    another operation x1, loops' own time, carried_in(): return lax.fori_loop(0, length, turn, start)  63.7 us
    dynamic_slice x96, local copies, waits for them, and re-layouts, turn(): new = combine(before, everything[k])  62.4 us
    ppermute x6, starting transfers between devices, from_behind(): lax.ppermute(array, axis, [(i, (i + by) % length) for i in range(length)])  23.2 us
    ppermute x6, waiting for transfers between devices, from_behind(): lax.ppermute(array, axis, [(i, (i + by) % length) for i in range(length)])  17 us
    all_to_all x1, waiting for transfers between devices, per_device(): lax.all_to_all(depth_sent, 'peer', split_axis=0, concat_axis=0, tiled=True)  8.97 us
  transfers between devices with their start and end apart: 9, of which 6 were waited for; matrix products, arithmetic and copies ran while one was open for 21% of the time, Pallas kernels for 0%

commit v1 on v0

v1 whole, which is shorter than its diff:
```python
import functools

import jax
import jax.numpy as jnp
from jax import lax
from jax.experimental import pallas as pl
from jax.experimental.pallas import tpu as pltpu
from jax.sharding import PartitionSpec as P

LEV = 48
SLOTS = 256
EDGE = 64
MICRO = 24
LANES = 128
MESH = pl.DeviceIdType.MESH
F32 = jnp.float32
BF16 = jnp.bfloat16


def mm(a, b):
    return lax.dot_general(a, b, (((1,), (0,)), ((), ())), preferred_element_type=F32)


def mm_nt(a, b):
    return lax.dot_general(a, b, (((1,), (1,)), ((), ())), preferred_element_type=F32)


def one_hot(condition):
    return jnp.where(condition, 1.0, 0.0).astype(BF16)


def iota(shape, dim):
    return lax.broadcasted_iota(jnp.int32, shape, dim)


def kernel(
    n_grp, n_peer,
    x_hbm, cost_hbm, links_hbm, wd_hbm, wr_hbm, wc_hbm,
    out,
    x, cost, links, wd, wr, wc,
    xb, wct, wdr, dt, pt, first, now, mask, rim_out, rim_in, edge_out, edge_in,
    load_sem, send_sem, recv_sem,
):
    width, cols = x.shape
    tiles = cols // LANES
    half = width // 2
    flat = lax.axis_index("grp") * n_peer + lax.axis_index("peer")
    count = n_grp * n_peer
    right = lax.rem(flat + 1, count)
    left = lax.rem(flat + count - 1, count)
    right_id = (lax.div(right, n_peer), lax.rem(right, n_peer))
    left_id = (lax.div(left, n_peer), lax.rem(left, n_peer))

    def lane_tile(t):
        return pl.ds(t * LANES, LANES)

    loads = {}
    order = [tiles - 1, 0] + list(range(1, tiles - 1))
    for t in order[:1]:
        loads[t] = pltpu.make_async_copy(x_hbm.at[:, lane_tile(t)], x.at[:, lane_tile(t)], load_sem.at[t])
        loads[t].start()

    barrier = pltpu.get_barrier_semaphore()
    pl.semaphore_signal(barrier, inc=1, device_id=left_id, device_id_type=MESH)

    for k, (src, dst) in enumerate(((links_hbm, links), (cost_hbm, cost))):
        loads["links" if k == 0 else "cost"] = pltpu.make_async_copy(src, dst, load_sem.at[tiles + k])
        loads["links" if k == 0 else "cost"].start()
    for t in order[1:]:
        loads[t] = pltpu.make_async_copy(x_hbm.at[:, lane_tile(t)], x.at[:, lane_tile(t)], load_sem.at[t])
        loads[t].start()
    for k, (name, src, dst) in enumerate((("wc", wc_hbm, wc), ("wd", wd_hbm, wd), ("wr", wr_hbm, wr))):
        loads[name] = pltpu.make_async_copy(src, dst, load_sem.at[tiles + 2 + k])
        loads[name].start()

    last = lane_tile(tiles - 1)
    loads[tiles - 1].wait()
    upper = pltpu.roll(x[:half, last], EDGE, 1)
    lower = x[half:, last]
    rim_out[...] = jnp.where(iota((half, LANES), 1) < EDGE, upper, lower).astype(BF16)
    pl.semaphore_wait(barrier, 1)
    forward = pltpu.make_async_remote_copy(
        src_ref=rim_out, dst_ref=rim_in, send_sem=send_sem.at[0], recv_sem=recv_sem.at[0],
        device_id=right_id, device_id_type=MESH,
    )
    forward.start()

    loads["links"].wait()
    link_row = jnp.concatenate([links[...], jnp.full((1, LANES - EDGE), -LANES, jnp.int32)], axis=1)
    rows_at = iota((LANES, LANES), 0)
    match_top = one_hot(rows_at == link_row)
    match_bottom = one_hot(rows_at - EDGE == link_row)

    for t in range(tiles):
        if t < tiles - 1:
            loads[t].wait()
        xb[:width, lane_tile(t)] = x[:, lane_tile(t)].astype(BF16)
    edge_out[...] = (
        mm_nt(xb[:half, :LANES], match_top) + mm_nt(xb[half:width, :LANES], match_bottom)
    ).astype(BF16)

    loads["cost"].wait()
    depth_row = cost[...]
    xb[width:, :] = jnp.broadcast_to(depth_row.astype(F32), (xb.shape[0] - width, cols)).astype(BF16)
    cloudy = jnp.where(depth_row > 0, 1.0, 0.0)
    cloudy_rows = jnp.broadcast_to(cloudy, (16, cols)).astype(BF16)
    ahead = one_hot(iota((LANES, LANES), 0) < iota((LANES, LANES), 1))
    before = jnp.zeros((1, 1), F32)
    for t in range(tiles):
        here = cloudy[:, t * LANES:(t + 1) * LANES]
        rank = mm(cloudy_rows[:, t * LANES:(t + 1) * LANES], ahead)[:1] + before
        before = before + jnp.sum(here, axis=1, keepdims=True)
        place = jnp.where(here > 0, rank.astype(jnp.int32), -1)
        pt[:, lane_tile(t)] = one_hot(iota((SLOTS, LANES), 0) == place)

    eye = one_hot(iota((width, width), 0) == iota((width, width), 1))
    loads["wc"].wait()
    wct[...] = mm_nt(eye, wc[...]).astype(BF16)

    gathered = mm_nt(xb[...], pt[...])
    first[...] = gathered[:width]
    now[...] = gathered[:width]
    slot_depth = gathered[width:width + 1].astype(jnp.int32)
    level = lax.rem(iota((width, SLOTS), 0), LEV)
    mask[...] = jnp.where(level >= LEV - slot_depth, 0.1, 0.0)

    def micro_turn(i, carry):
        forcing = mm(wct[...], now[...].astype(BF16))
        now[...] = now[...] + mask[...] * jnp.tanh(forcing)
        return carry

    lax.fori_loop(0, MICRO, micro_turn, 0)
    change = (now[...] - first[...]).astype(BF16)

    loads["wd"].wait()
    loads["wr"].wait()
    wdr[:width] = mm_nt(eye, wd[...]).astype(BF16)
    wdr[width:] = mm_nt(eye, wr[...]).astype(BF16)
    wdt = wdr[:width]
    two = mm(wdt, wdt)
    three = mm(wdt, two.astype(BF16))
    dt[...] = (0.6 * wdt.astype(F32) + 0.12 * two + 0.008 * three).astype(BF16)

    for t in range(tiles):
        at = lane_tile(t)
        both = mm(wdr[...], xb[:width, at])
        turned = x[:, at] + 0.2 * both[:width]
        rest = 0.25 * both[width:] + mm(change, pt[:, at])
        for _ in range(2):
            turned = turned + 0.2 * mm(wdr[:width], turned.astype(BF16))
        lane = iota((width, LANES), 1)
        if t == 0:
            turned = jnp.where(lane < EDGE, 0.5 * turned, turned)
        if t == tiles - 1:
            turned = jnp.where(lane >= EDGE, 0.5 * turned, turned)
        out[:, at] = turned + rest

    forward.wait_recv()
    backward = pltpu.make_async_remote_copy(
        src_ref=edge_out, dst_ref=edge_in, send_sem=send_sem.at[1], recv_sem=recv_sem.at[1],
        device_id=left_id, device_id_type=MESH,
    )
    backward.start()
    matched = jnp.concatenate([mm(rim_in[...], match_top), mm(rim_in[...], match_bottom)], axis=0)
    out[:, :LANES] = out[:, :LANES] + 0.5 * (matched + mm(dt[...], matched.astype(BF16)))

    backward.wait_recv()
    into_top = one_hot((iota((LANES, LANES), 0) + EDGE == iota((LANES, LANES), 1)))
    into_bottom = one_hot((iota((LANES, LANES), 0) == iota((LANES, LANES), 1)) & (iota((LANES, LANES), 0) >= EDGE))
    matched = jnp.concatenate([mm(edge_in[...], into_top), mm(edge_in[...], into_bottom)], axis=0)
    out[:, last] = out[:, last] + 0.5 * (matched + mm(dt[...], matched.astype(BF16)))
    forward.wait_send()
    backward.wait_send()


def solution(mesh):
    n_grp, n_peer = mesh.shape["grp"], mesh.shape["peer"]

    def per_device(state, cost, links, dyn_weight, rad_weight, cloud_weight):
        cols, width = state.shape
        half = width // 2
        tiles = cols // LANES
        flipped = pl.pallas_call(
            functools.partial(kernel, n_grp, n_peer),
            out_shape=jax.ShapeDtypeStruct((width, cols), F32),
            in_specs=[pl.BlockSpec(memory_space=pltpu.HBM)] * 6,
            out_specs=pl.BlockSpec(memory_space=pltpu.VMEM),
            scratch_shapes=[
                pltpu.VMEM((width, cols), F32),
                pltpu.VMEM((1, cols), jnp.int32),
                pltpu.VMEM((1, EDGE), jnp.int32),
                pltpu.VMEM((width, width), BF16),
                pltpu.VMEM((width, width), BF16),
                pltpu.VMEM((width, width), BF16),
                pltpu.VMEM((width + 16, cols), BF16),
                pltpu.VMEM((width, width), BF16),
                pltpu.VMEM((2 * width, width), BF16),
                pltpu.VMEM((width, width), BF16),
                pltpu.VMEM((SLOTS, cols), BF16),
                pltpu.VMEM((width, SLOTS), F32),
                pltpu.VMEM((width, SLOTS), F32),
                pltpu.VMEM((width, SLOTS), F32),
                pltpu.VMEM((half, LANES), BF16),
                pltpu.VMEM((half, LANES), BF16),
                pltpu.VMEM((half, LANES), BF16),
                pltpu.VMEM((half, LANES), BF16),
                pltpu.SemaphoreType.DMA((tiles + 5,)),
                pltpu.SemaphoreType.DMA((2,)),
                pltpu.SemaphoreType.DMA((2,)),
            ],
            compiler_params=pltpu.CompilerParams(
                collective_id=0, has_side_effects=True, vmem_limit_bytes=32 * 2**20
            ),
        )(state.T, cost.reshape(1, cols), links, dyn_weight, rad_weight, cloud_weight)
        return flipped.T

    return jax.shard_map(
        per_device,
        mesh=mesh,
        in_specs=(
            P(("grp", "peer"), None),
            P(("grp", "peer")),
            P(("grp", "peer"), None),
            P(),
            P(),
            P(),
        ),
        out_specs=P(("grp", "peer"), None),
        check_vma=False,
    )
```

time: 447 us -> 25.9 us (0.06); the launches traced: 440 us -> 25.6 us
  blocking collectives: 200 us -> 0 us
  local copies, waits for them, and re-layouts: 84.4 us -> 5.37 us
  loops' own time: 64.5 us -> 0 us
  starting transfers between devices: 41.3 us -> 0 us
  waiting for transfers between devices: 30.3 us -> 0 us
  Pallas kernels: 0 us -> 20.2 us
  other arithmetic: 13.7 us -> 0 us
  matrix products: 5.55 us -> 0 us
    unnamed x1 -> x0, blocking collectives: 200 us -> none
    another operation x2 -> x0, loops' own time: 64.5 us -> none  [the longest x1 63.7 us: carried_in(): return lax.fori_loop(0, length, turn, start)]
    dynamic_slice x96 -> x0, local copies, waits for them, and re-layouts: 62.4 us -> none  [turn(): new = combine(before, everything[k])]
    ppermute x6 -> x0, starting transfers between devices: 23.2 us -> none  [from_behind(): lax.ppermute(array, axis, [(i, (i + by) % length) for i in range(length)])]
    pallas_call x0 -> x1, Pallas kernels: none -> 20.2 us  [per_device(): pl.pallas_call(functools.partial(kernel, n_grp, n_peer), out_shape=jax.Sh...]
    all_to_all x3 -> x0, starting transfers between devices: 18.2 us -> none  [the longest x1 6.28 us: per_device(): lax.all_to_all(depth_sent, 'peer', split_axis=0, concat_axis=0, tiled=True)]
    ppermute x6 -> x0, waiting for transfers between devices: 17 us -> none  [from_behind(): lax.ppermute(array, axis, [(i, (i + by) % length) for i in range(length)])]
    all_to_all x3 -> x0, waiting for transfers between devices: 13.3 us -> none  [the longest x1 8.97 us: per_device(): lax.all_to_all(depth_sent, 'peer', split_axis=0, concat_axis=0, tiled=True)]
  transfers between devices with their start and end apart: 9 -> 0, of which waited for: 6 -> 0; matrix products, arithmetic and copies ran while one was open for 21% -> 0% of each run, Pallas kernels for 0% -> 0%
where the time goes in v1:
time: 25.9 us; the launch traced here: 25.6 us
  Pallas kernels  20.2 us (78%)
  local copies, waits for them, and re-layouts  5.37 us (21%)
    pallas_call x1, Pallas kernels, per_device(): pl.pallas_call(functools.partial(kernel, n_grp, n_peer), out_shape=jax.Sh...  20.2 us
    unnamed x13, local copies, waits for them, and re-layouts  5.37 us

profile of v1, /device:TPU:56, one launch (start us, length us, event | category | flops | bytes accessed | tf_op | source)
XLA Modules:
  0.0 25.6 jit_solution(9382297607402866347)
XLA Ops:
  0.0 0.0 copy-start.4
  0.0 0.0 copy-start.5
  0.0 0.7 %copy-done.4 = s32[512]{0:T(512)S(1)} copy-done((s32[512]{0:T(512)S(1)}, s32[512]{0:T(512)}, u32[]{:S(2)}) %copy-start.4) | copy-done | bytes 2072
  0.7 0.0 copy-done.5
  0.7 0.0 copy-start
  0.7 1.1 %copy-done = f32[512,288]{0,1:T(8,128)S(1)} copy-done((f32[512,288]{0,1:T(8,128)S(1)}, f32[512,288]{0,1:T(8,128)}, u32[]{:S(2)}) %copy-start) | copy-done | bytes 589848
  1.8 0.0 copy-start.1
  1.8 0.9 %copy-done.1 = bf16[288,288]{1,0:T(8,128)(2,1)S(1)} copy-done((bf16[288,288]{1,0:T(8,128)(2,1)S(1)}, bf16[288,288]{1,0:T(8,128)(2,1)}, u32[]{:S(2)}) %copy-start.1) | copy-done | bytes 165912
  2.7 0.0 copy-start.2
  2.7 0.9 %copy-done.2 = bf16[288,288]{1,0:T(8,128)(2,1)S(1)} copy-done((bf16[288,288]{1,0:T(8,128)(2,1)S(1)}, bf16[288,288]{1,0:T(8,128)(2,1)}, u32[]{:S(2)}) %copy-start.2) | copy-done | bytes 165912
  3.6 0.0 copy-start.3
  3.6 0.9 %copy-done.3 = bf16[288,288]{1,0:T(8,128)(2,1)S(1)} copy-done((bf16[288,288]{1,0:T(8,128)(2,1)S(1)}, bf16[288,288]{1,0:T(8,128)(2,1)}, u32[]{:S(2)}) %copy-start.3) | copy-done | bytes 165912
  4.6 20.2 %shard_map.64 = f32[288,512]{1,0:T(8,128)S(1)} custom-call(f32[288,512]{1,0:T(8,128)S(1)} %bitcast.4, s32[1,512]{1,0:T(1,128)S(1)} %bitcast.5, s32[1,64]{1,0:T(1,128)S(1)} %copy-done.5, bf16[288,288]{1,0:T(8,128)(2,1)S(1)} %copy-done.1, bf16[288,288]{1,0:T(8,128)(2,1)S(1)} %copy-done.2, bf16[288,288]{1,0:T(8,128)(2,1)S(1)} %copy-done.3), custom_call_target="tpu_custom_call" | custom-call | tf_op jit(solution)/shard_map/pallas_call | solution.py:183
  24.8 0.8 %copy.8 = f32[512,288]{0,1:T(8,128)} copy(f32[512,288]{0,1:T(8,128)S(1)} %bitcast.3) | data formatting | bytes 1179648
Async XLA Ops:
  0.0 0.7 %copy-start.4 = (s32[512]{0:T(512)S(1)}, s32[512]{0:T(512)}, u32[]{:S(2)}) copy-start(s32[512]{0:T(512)} %param.7) | copy-start | bytes 6148
  0.0 0.7 %copy-start.5 = (s32[1,64]{1,0:T(1,128)S(1)}, s32[1,64]{1,0:T(1,128)}, u32[]{:S(2)}) copy-start(s32[1,64]{1,0:T(1,128)} %links_hbm.1) | copy-start | bytes 772
  0.7 1.1 %copy-start = (f32[512,288]{0,1:T(8,128)S(1)}, f32[512,288]{0,1:T(8,128)}, u32[]{:S(2)}) copy-start(f32[512,288]{0,1:T(8,128)} %param.6) | copy-start | bytes 1769476
  1.8 0.9 %copy-start.1 = (bf16[288,288]{1,0:T(8,128)(2,1)S(1)}, bf16[288,288]{1,0:T(8,128)(2,1)}, u32[]{:S(2)}) copy-start(bf16[288,288]{1,0:T(8,128)(2,1)} %wd_hbm.1) | copy-start | bytes 497668
  2.7 0.9 %copy-start.2 = (bf16[288,288]{1,0:T(8,128)(2,1)S(1)}, bf16[288,288]{1,0:T(8,128)(2,1)}, u32[]{:S(2)}) copy-start(bf16[288,288]{1,0:T(8,128)(2,1)} %wr_hbm.1) | copy-start | bytes 497668
  3.6 0.9 %copy-start.3 = (bf16[288,288]{1,0:T(8,128)(2,1)S(1)}, bf16[288,288]{1,0:T(8,128)(2,1)}, u32[]{:S(2)}) copy-start(bf16[288,288]{1,0:T(8,128)(2,1)} %wc_hbm.1) | copy-start | bytes 497668

commit v2 on v1

v2 whole, which is shorter than its diff:
```python
import functools

import jax
import jax.numpy as jnp
from jax import lax
from jax.experimental import pallas as pl
from jax.experimental.pallas import tpu as pltpu
from jax.sharding import PartitionSpec as P

LEV = 48
SLOTS = 256
EDGE = 64
MICRO = 24
LANES = 128
WIDE = 256
PIECES = 3
MESH = pl.DeviceIdType.MESH
F32 = jnp.float32
BF16 = jnp.bfloat16


def mm(a, b):
    return lax.dot_general(a, b, (((1,), (0,)), ((), ())), preferred_element_type=F32)


def mm_nt(a, b):
    return lax.dot_general(a, b, (((1,), (1,)), ((), ())), preferred_element_type=F32)


def one_hot(condition):
    return jnp.where(condition, 1.0, 0.0).astype(BF16)


def iota(shape, dim):
    return lax.broadcasted_iota(jnp.int32, shape, dim)


def kernel(
    n_grp, n_peer,
    x_hbm, cost_hbm, links_hbm, wd_hbm, wr_hbm, wc_hbm,
    out,
    x, cost, links, wd, wr, wc,
    xb, wct, wdr, dt, pt, match, first, now, mask, rim_out, rim_in, edge_out, edge_in,
    rim_sem, load_sem, send_sem, recv_sem, ready_sem,
):
    width, cols = x.shape
    first_peer = lax.axis_index("peer") == 0
    tiles = cols // LANES
    half = width // 2
    flat = lax.axis_index("grp") * n_peer + lax.axis_index("peer")
    count = n_grp * n_peer
    right = lax.rem(flat + 1, count)
    left = lax.rem(flat + count - 1, count)
    right_id = (lax.div(right, n_peer), lax.rem(right, n_peer))
    left_id = (lax.div(left, n_peer), lax.rem(left, n_peer))

    def lane_tile(t):
        return pl.ds(t * LANES, LANES)

    last = lane_tile(tiles - 1)
    piece = half // PIECES
    pieces = [pl.ds(k * piece, piece) for k in range(PIECES)]
    rim_loads = []
    for k in range(PIECES):
        for side in range(2):
            rows = pl.ds(side * half + k * piece, piece)
            rim_loads.append(pltpu.make_async_copy(x_hbm.at[rows, last], x.at[rows, last], rim_sem.at[2 * k + side]))
            rim_loads[-1].start()

    barrier = pltpu.get_barrier_semaphore()
    pl.semaphore_signal(barrier, inc=1, device_id=left_id, device_id_type=MESH)

    loads = {}
    for k, (name, src, dst) in enumerate((
        ("links", links_hbm, links),
        (0, x_hbm.at[:, lane_tile(0)], x.at[:, lane_tile(0)]),
        ("cost", cost_hbm, cost),
        (1, x_hbm.at[:, pl.ds(LANES, cols - 2 * LANES)], x.at[:, pl.ds(LANES, cols - 2 * LANES)]),
        ("wc", wc_hbm, wc),
        ("wd", wd_hbm, wd),
        ("wr", wr_hbm, wr),
    )):
        loads[name] = pltpu.make_async_copy(src, dst, load_sem.at[k])
        loads[name].start()

    pl.semaphore_wait(barrier, 1)
    pl.semaphore_signal(ready_sem, inc=1, device_id=right_id, device_id_type=MESH)

    forward = []
    for k in range(PIECES):
        rim_loads[2 * k].wait()
        rim_loads[2 * k + 1].wait()
        upper = pltpu.roll(x[pieces[k], last], EDGE, 1)
        lower = x[pl.ds(half + k * piece, piece), last]
        rim_out[pieces[k]] = jnp.where(iota((piece, LANES), 1) < EDGE, upper, lower).astype(BF16)
        forward.append(pltpu.make_async_remote_copy(
            src_ref=rim_out.at[pieces[k]], dst_ref=rim_in.at[pieces[k]],
            send_sem=send_sem.at[k], recv_sem=recv_sem.at[k],
            device_id=right_id, device_id_type=MESH,
        ))
        forward[k].start()
    backward = pltpu.make_async_remote_copy(
        src_ref=edge_out, dst_ref=edge_in, send_sem=send_sem.at[PIECES], recv_sem=recv_sem.at[PIECES],
        device_id=left_id, device_id_type=MESH,
    )

    loads["links"].wait()
    link_row = jnp.concatenate([links[...], jnp.full((1, LANES - EDGE), -LANES, jnp.int32)], axis=1)
    rows_at = iota((LANES, LANES), 0)
    match[:, :LANES] = one_hot(rows_at == link_row)
    match[:, LANES:] = one_hot(rows_at - EDGE == link_row)

    loads[0].wait()
    xb[:width, :LANES] = x[:, :LANES].astype(BF16)
    edge_out[...] = (
        mm_nt(xb[:half, :LANES], match[:, :LANES]) + mm_nt(xb[half:width, :LANES], match[:, LANES:])
    ).astype(BF16)
    loads[1].wait()
    for t in range(1, tiles):
        xb[:width, lane_tile(t)] = x[:, lane_tile(t)].astype(BF16)

    loads["cost"].wait()
    depth_row = cost[...]
    xb[width:, :] = jnp.broadcast_to(depth_row.astype(F32), (xb.shape[0] - width, cols)).astype(BF16)
    cloudy = jnp.where(depth_row > 0, 1.0, 0.0)
    cloudy_rows = jnp.broadcast_to(cloudy, (16, cols)).astype(BF16)
    ahead = one_hot(iota((LANES, LANES), 0) < iota((LANES, LANES), 1))
    before = jnp.zeros((1, 1), F32)
    for t in range(tiles):
        here = cloudy[:, t * LANES:(t + 1) * LANES]
        rank = mm(cloudy_rows[:, t * LANES:(t + 1) * LANES], ahead)[:1] + before
        before = before + jnp.sum(here, axis=1, keepdims=True)
        place = jnp.where(here > 0, rank.astype(jnp.int32), -1)
        pt[:, lane_tile(t)] = one_hot(iota((SLOTS, LANES), 0) == place)

    eye = one_hot(iota((width, width), 0) == iota((width, width), 1))
    loads["wc"].wait()
    wct[...] = mm_nt(eye, wc[...]).astype(BF16)

    gathered = mm_nt(xb[...], pt[...])
    first[...] = gathered[:width]
    now[...] = gathered[:width]
    slot_depth = gathered[width:width + 1].astype(jnp.int32)
    level = lax.rem(iota((width, SLOTS), 0), LEV)
    mask[...] = jnp.where(level >= LEV - slot_depth, 0.1, 0.0)

    def micro_turn(i, carry):
        forcing = mm(wct[...], now[...].astype(BF16))
        now[...] = now[...] + mask[...] * jnp.tanh(forcing)
        return carry

    lax.fori_loop(0, MICRO, micro_turn, 0)
    change = (now[...] - first[...]).astype(BF16)

    @pl.when(jnp.logical_not(first_peer))
    def _():
        pl.semaphore_wait(ready_sem, 1)
        backward.start()

    loads["wd"].wait()
    loads["wr"].wait()
    wdr[:width] = mm_nt(eye, wd[...]).astype(BF16)
    wdr[width:] = mm_nt(eye, wr[...]).astype(BF16)
    wdt = wdr[:width]
    two = mm(wdt, wdt)
    three = mm(wdt, two.astype(BF16))
    dt[...] = (0.6 * wdt.astype(F32) + 0.12 * two + 0.008 * three).astype(BF16)

    for t in range(cols // WIDE):
        at = pl.ds(t * WIDE, WIDE)
        both = mm(wdr[...], xb[:width, at])
        turned = x[:, at] + 0.2 * both[:width]
        rest = 0.25 * both[width:] + mm(change, pt[:, at])
        for _ in range(2):
            turned = turned + 0.2 * mm(wdr[:width], turned.astype(BF16))
        column = iota((width, WIDE), 1) + t * WIDE
        turned = jnp.where((column < EDGE) | (column >= cols - EDGE), 0.5 * turned, turned)
        out[:, at] = turned + rest

    backward.wait_recv()
    above, across = iota((LANES, LANES), 0), iota((LANES, LANES), 1)
    into_top = one_hot(above + EDGE == across)
    into_bottom = one_hot((above == across) & (above >= EDGE))
    matched = jnp.concatenate([mm(edge_in[...], into_top), mm(edge_in[...], into_bottom)], axis=0)
    out[:, last] = out[:, last] + 0.5 * (matched + mm(dt[...], matched.astype(BF16)))

    @pl.when(first_peer)
    def _():
        pl.semaphore_wait(ready_sem, 1)
        backward.start()

    for copy in forward:
        copy.wait_recv()
    halves = mm(rim_in[...], match[...])
    matched = jnp.concatenate([halves[:, :LANES], halves[:, LANES:]], axis=0)
    out[:, :LANES] = out[:, :LANES] + 0.5 * (matched + mm(dt[...], matched.astype(BF16)))
    for copy in forward:
        copy.wait_send()
    backward.wait_send()


def solution(mesh):
    n_grp, n_peer = mesh.shape["grp"], mesh.shape["peer"]

    def per_device(state, cost, links, dyn_weight, rad_weight, cloud_weight):
        cols, width = state.shape
        half = width // 2
        held = [state.T, cost.reshape(1, cols), links, dyn_weight, rad_weight, cloud_weight]
        held = [pltpu.with_memory_space_constraint(one, pltpu.HBM) for one in held]
        flipped = pl.pallas_call(
            functools.partial(kernel, n_grp, n_peer),
            out_shape=jax.ShapeDtypeStruct((width, cols), F32),
            in_specs=[pl.BlockSpec(memory_space=pltpu.HBM)] * 6,
            out_specs=pl.BlockSpec(memory_space=pltpu.VMEM),
            scratch_shapes=[
                pltpu.VMEM((width, cols), F32),
                pltpu.VMEM((1, cols), jnp.int32),
                pltpu.VMEM((1, EDGE), jnp.int32),
                pltpu.VMEM((width, width), BF16),
                pltpu.VMEM((width, width), BF16),
                pltpu.VMEM((width, width), BF16),
                pltpu.VMEM((width + 16, cols), BF16),
                pltpu.VMEM((width, width), BF16),
                pltpu.VMEM((2 * width, width), BF16),
                pltpu.VMEM((width, width), BF16),
                pltpu.VMEM((SLOTS, cols), BF16),
                pltpu.VMEM((LANES, 2 * LANES), BF16),
                pltpu.VMEM((width, SLOTS), F32),
                pltpu.VMEM((width, SLOTS), F32),
                pltpu.VMEM((width, SLOTS), F32),
                pltpu.VMEM((half, LANES), BF16),
                pltpu.VMEM((half, LANES), BF16),
                pltpu.VMEM((half, LANES), BF16),
                pltpu.VMEM((half, LANES), BF16),
                pltpu.SemaphoreType.DMA((2 * PIECES,)),
                pltpu.SemaphoreType.DMA((7,)),
                pltpu.SemaphoreType.DMA((PIECES + 1,)),
                pltpu.SemaphoreType.DMA((PIECES + 1,)),
                pltpu.SemaphoreType.REGULAR,
            ],
            compiler_params=pltpu.CompilerParams(
                collective_id=0, has_side_effects=True, vmem_limit_bytes=32 * 2**20
            ),
        )(*held)
        return flipped.T

    return jax.shard_map(
        per_device,
        mesh=mesh,
        in_specs=(
            P(("grp", "peer"), None),
            P(("grp", "peer")),
            P(("grp", "peer"), None),
            P(),
            P(),
            P(),
        ),
        out_specs=P(("grp", "peer"), None),
        check_vma=False,
    )
```

time: 25.9 us -> 19.8 us (0.76)
  local copies, waits for them, and re-layouts: 5.37 us -> 0.82 us
  Pallas kernels: 20.2 us -> 18.9 us
    unnamed x13 -> x1, local copies, waits for them, and re-layouts: 5.37 us -> 0.82 us
    pallas_call x1, Pallas kernels: 20.2 us -> 18.9 us  [per_device(): pl.pallas_call(functools.partial(kernel, n_grp, n_peer), out_shape=jax.Sh...]
where the time goes in v2:
time: 19.8 us; the launch traced here: 19.7 us
  Pallas kernels  18.9 us (95%)
  local copies, waits for them, and re-layouts  0.82 us (4%)
    pallas_call x1, Pallas kernels, per_device(): pl.pallas_call(functools.partial(kernel, n_grp, n_peer), out_shape=jax.Sh...  18.9 us
    unnamed x1, local copies, waits for them, and re-layouts  0.82 us

profile of v2, /device:TPU:56, one launch (start us, length us, event | category | flops | bytes accessed | tf_op | source)
XLA Modules:
  0.0 19.7 jit_solution(16651200474865792112)
XLA Ops:
  0.0 18.9 %shard_map.64 = f32[288,512]{1,0:T(8,128)S(1)} custom-call(f32[288,512]{1,0:T(8,128)} %bitcast.4, s32[1,512]{1,0:T(1,128)} %bitcast.5, s32[1,64]{1,0:T(1,128)} %links_hbm.1, bf16[288,288]{1,0:T(8,128)(2,1)} %wd_hbm.1, bf16[288,288]{1,0:T(8,128)(2,1)} %wr_hbm.1, bf16[288,288]{1,0:T(8,128)(2,1)} %wc_hbm.1), custom_call_target="tpu_custom_call" | custom-call | tf_op jit(solution)/shard_map/pallas_call | solution.py:210
  18.9 0.8 %copy.8 = f32[512,288]{0,1:T(8,128)} copy(f32[512,288]{0,1:T(8,128)S(1)} %bitcast.3) | data formatting | bytes 1179648

commit v3 on v2

--- a/solution.py
+++ b/solution.py
@@ -38,9 +38,9 @@
 def kernel(
     n_grp, n_peer,
     x_hbm, cost_hbm, links_hbm, wd_hbm, wr_hbm, wc_hbm,
-    out,
+    out, came, spot, dt,
     x, cost, links, wd, wr, wc,
-    xb, wct, wdr, dt, pt, match, first, now, mask, rim_out, rim_in, edge_out, edge_in,
+    xb, wct, wdr, pt, first, now, mask, rim_out, rim_in, edge_out, edge_in,
     rim_sem, load_sem, send_sem, recv_sem, ready_sem,
 ):
     width, cols = x.shape
@@ -107,13 +107,14 @@
     loads["links"].wait()
     link_row = jnp.concatenate([links[...], jnp.full((1, LANES - EDGE), -LANES, jnp.int32)], axis=1)
     rows_at = iota((LANES, LANES), 0)
-    match[:, :LANES] = one_hot(rows_at == link_row)
-    match[:, LANES:] = one_hot(rows_at - EDGE == link_row)
+    match_top = one_hot(rows_at == link_row)
+    match_bottom = one_hot(rows_at - EDGE == link_row)
+    spot[...] = jnp.concatenate([links[...], links[...] + EDGE], axis=1)
 
     loads[0].wait()
     xb[:width, :LANES] = x[:, :LANES].astype(BF16)
     edge_out[...] = (
-        mm_nt(xb[:half, :LANES], match[:, :LANES]) + mm_nt(xb[half:width, :LANES], match[:, LANES:])
+        mm_nt(xb[:half, :LANES], match_top) + mm_nt(xb[half:width, :LANES], match_bottom)
     ).astype(BF16)
     loads[1].wait()
     for t in range(1, tiles):
@@ -191,12 +192,31 @@
 
     for copy in forward:
         copy.wait_recv()
-    halves = mm(rim_in[...], match[...])
-    matched = jnp.concatenate([halves[:, :LANES], halves[:, LANES:]], axis=0)
-    out[:, :LANES] = out[:, :LANES] + 0.5 * (matched + mm(dt[...], matched.astype(BF16)))
+    came[...] = rim_in[...]
     for copy in forward:
         copy.wait_send()
     backward.wait_send()
+
+
+def finish(part, came, spot, dt, out, left, sem):
+    rest = pltpu.make_async_copy(part.at[:, LANES:], out.at[:, LANES:], sem.at[0])
+    rest.start()
+    half = came.shape[0]
+    width = 2 * half
+    found = jnp.take_along_axis(came[...].astype(F32), jnp.broadcast_to(spot[...], (half, LANES)), axis=1)
+    matched = jnp.concatenate([found, pltpu.roll(found, EDGE, 1)], axis=0)
+    matched = jnp.where(iota((width, LANES), 1) < EDGE, matched, 0.0)
+    rounded = matched.astype(BF16)
+    copies = [rest]
+    rows = width // PIECES
+    for k in range(PIECES):
+        at = slice(k * rows, (k + 1) * rows)
+        left[at] = part[at, :LANES] + 0.5 * (matched[at] + mm(dt[at], rounded))
+        here = pl.ds(k * rows, rows)
+        copies.append(pltpu.make_async_copy(left.at[here], out.at[here, :LANES], sem.at[1 + k]))
+        copies[-1].start()
+    for copy in copies:
+        copy.wait()
 
 
 def solution(mesh):
@@ -207,11 +227,16 @@
         half = width // 2
         held = [state.T, cost.reshape(1, cols), links, dyn_weight, rad_weight, cloud_weight]
         held = [pltpu.with_memory_space_constraint(one, pltpu.HBM) for one in held]
-        flipped = pl.pallas_call(
+        parts = pl.pallas_call(
             functools.partial(kernel, n_grp, n_peer),
-            out_shape=jax.ShapeDtypeStruct((width, cols), F32),
+            out_shape=[
+                jax.ShapeDtypeStruct((width, cols), F32),
+                jax.ShapeDtypeStruct((half, LANES), BF16),
+                jax.ShapeDtypeStruct((1, LANES), jnp.int32),
+                jax.ShapeDtypeStruct((width, width), BF16),
+            ],
             in_specs=[pl.BlockSpec(memory_space=pltpu.HBM)] * 6,
-            out_specs=pl.BlockSpec(memory_space=pltpu.VMEM),
+            out_specs=[pl.BlockSpec(memory_space=pltpu.VMEM)] * 4,
             scratch_shapes=[
                 pltpu.VMEM((width, cols), F32),
                 pltpu.VMEM((1, cols), jnp.int32),
@@ -222,9 +247,7 @@
                 pltpu.VMEM((width + 16, cols), BF16),
                 pltpu.VMEM((width, width), BF16),
                 pltpu.VMEM((2 * width, width), BF16),
-                pltpu.VMEM((width, width), BF16),
                 pltpu.VMEM((SLOTS, cols), BF16),
-                pltpu.VMEM((LANES, 2 * LANES), BF16),
                 pltpu.VMEM((width, SLOTS), F32),
                 pltpu.VMEM((width, SLOTS), F32),
                 pltpu.VMEM((width, SLOTS), F32),
@@ -242,6 +265,14 @@
                 collective_id=0, has_side_effects=True, vmem_limit_bytes=32 * 2**20
             ),
         )(*held)
+        flipped = pl.pallas_call(
+            finish,
+            out_shape=jax.ShapeDtypeStruct((width, cols), F32),
+            in_specs=[pl.BlockSpec(memory_space=pltpu.VMEM)] * 4,
+            out_specs=pl.BlockSpec(memory_space=pltpu.HBM),
+            scratch_shapes=[pltpu.VMEM((width, LANES), F32), pltpu.SemaphoreType.DMA((1 + PIECES,))],
+            compiler_params=pltpu.CompilerParams(vmem_limit_bytes=8 * 2**20),
+        )(*[pltpu.with_memory_space_constraint(one, pltpu.VMEM) for one in parts])
         return flipped.T
 
     return jax.shard_map(

time: 19.8 us -> 19.6 us (0.990)
  local copies, waits for them, and re-layouts: 0.82 us -> 0 us
  Pallas kernels: 18.9 us -> 19.5 us
    unnamed x1 -> x0, local copies, waits for them, and re-layouts: 0.82 us -> none
    pallas_call x1 -> x2, Pallas kernels: 18.9 us -> 19.5 us  [the longest x1 18.5 us: per_device(): pl.pallas_call(functools.partial(kernel, n_grp, n_peer), out_shape=[jax.S...]
where the time goes in v3:
time: 19.6 us; the launch traced here: 19.5 us
  Pallas kernels  19.5 us (99%)
    pallas_call x1, Pallas kernels, per_device(): pl.pallas_call(functools.partial(kernel, n_grp, n_peer), out_shape=[jax.S...  18.5 us
    pallas_call x1, Pallas kernels, per_device(): pl.pallas_call(finish, out_shape=jax.ShapeDtypeStruct((width, cols), F32)...  1 us

profile of v3, /device:TPU:56, one launch (start us, length us, event | category | flops | bytes accessed | tf_op | source)
XLA Modules:
  0.0 19.5 jit_solution(11532727688237147366)
XLA Ops:
  0.0 18.5 %shard_map.64 = (f32[288,512]{1,0:T(8,128)S(1)}, bf16[144,128]{1,0:T(8,128)(2,1)S(1)}, s32[1,128]{1,0:T(1,128)S(1)}, bf16[288,288]{1,0:T(8,128)(2,1)S(1)}) custom-call(f32[288,512]{1,0:T(8,128)} %bitcast.3, s32[1,512]{1,0:T(1,128)} %bitcast.4, s32[1,64]{1,0:T(1,128)} %links_hbm.1, bf16[288,288]{1,0:T(8,128)(2,1)} %wd_hbm.1, bf16[288,288]{1,0:T(8,128)(2,1)} %wr_hbm.1, ...), custom_call_target="tpu_custom_call" | custom-call | tf_op jit(solution)/shard_map/pallas_call | solution.py:230
  18.5 1.0 %shard_map.65 = f32[288,512]{1,0:T(8,128)} custom-call(f32[288,512]{1,0:T(8,128)S(1)} %get-tuple-element.9.part, bf16[144,128]{1,0:T(8,128)(2,1)S(1)} %get-tuple-element.10.came, s32[1,128]{1,0:T(1,128)S(1)} %get-tuple-element.11.spot, bf16[288,288]{1,0:T(8,128)(2,1)S(1)} %get-tuple-element.12.dt), custom_call_target="tpu_custom_call" | custom-call | tf_op jit(solution)/shard_map/pallas_call | solution.py:268

commit v4 on v3

--- a/solution.py
+++ b/solution.py
@@ -13,7 +13,8 @@
 MICRO = 24
 LANES = 128
 WIDE = 256
-PIECES = 3
+PIECES = 2
+PIECE = 48
 MESH = pl.DeviceIdType.MESH
 F32 = jnp.float32
 BF16 = jnp.bfloat16
@@ -38,9 +39,9 @@
 def kernel(
     n_grp, n_peer,
     x_hbm, cost_hbm, links_hbm, wd_hbm, wr_hbm, wc_hbm,
-    out, came, spot, dt,
+    out, came, came_plain, spot, dt,
     x, cost, links, wd, wr, wc,
-    xb, wct, wdr, pt, first, now, mask, rim_out, rim_in, edge_out, edge_in,
+    xb, wct, wdr, pt, first, now, mask, rim_out, rim_in, plain_in, edge_out, edge_in,
     rim_sem, load_sem, send_sem, recv_sem, ready_sem,
 ):
     width, cols = x.shape
@@ -58,17 +59,27 @@
         return pl.ds(t * LANES, LANES)
 
     last = lane_tile(tiles - 1)
-    piece = half // PIECES
-    pieces = [pl.ds(k * piece, piece) for k in range(PIECES)]
+    packed = PIECES * PIECE
+    plain = width - 2 * packed
     rim_loads = []
     for k in range(PIECES):
         for side in range(2):
-            rows = pl.ds(side * half + k * piece, piece)
+            rows = pl.ds(plain + side * packed + k * PIECE, PIECE)
             rim_loads.append(pltpu.make_async_copy(x_hbm.at[rows, last], x.at[rows, last], rim_sem.at[2 * k + side]))
             rim_loads[-1].start()
 
     barrier = pltpu.get_barrier_semaphore()
     pl.semaphore_signal(barrier, inc=1, device_id=left_id, device_id_type=MESH)
+
+    pl.semaphore_wait(barrier, 1)
+    pl.semaphore_signal(ready_sem, inc=1, device_id=right_id, device_id_type=MESH)
+
+    forward = [pltpu.make_async_remote_copy(
+        src_ref=x_hbm.at[pl.ds(0, plain), last], dst_ref=plain_in,
+        send_sem=send_sem.at[PIECES + 1], recv_sem=recv_sem.at[PIECES + 1],
+        device_id=right_id, device_id_type=MESH,
+    )]
+    forward[0].start()
 
     loads = {}
     for k, (name, src, dst) in enumerate((
@@ -76,6 +87,7 @@
         (0, x_hbm.at[:, lane_tile(0)], x.at[:, lane_tile(0)]),
         ("cost", cost_hbm, cost),
         (1, x_hbm.at[:, pl.ds(LANES, cols - 2 * LANES)], x.at[:, pl.ds(LANES, cols - 2 * LANES)]),
+        (2, x_hbm.at[pl.ds(0, plain), last], x.at[pl.ds(0, plain), last]),
         ("wc", wc_hbm, wc),
         ("wd", wd_hbm, wd),
         ("wr", wr_hbm, wr),
@@ -83,22 +95,19 @@
         loads[name] = pltpu.make_async_copy(src, dst, load_sem.at[k])
         loads[name].start()
 
-    pl.semaphore_wait(barrier, 1)
-    pl.semaphore_signal(ready_sem, inc=1, device_id=right_id, device_id_type=MESH)
-
-    forward = []
     for k in range(PIECES):
         rim_loads[2 * k].wait()
         rim_loads[2 * k + 1].wait()
-        upper = pltpu.roll(x[pieces[k], last], EDGE, 1)
-        lower = x[pl.ds(half + k * piece, piece), last]
-        rim_out[pieces[k]] = jnp.where(iota((piece, LANES), 1) < EDGE, upper, lower).astype(BF16)
+        here = pl.ds(k * PIECE, PIECE)
+        upper = pltpu.roll(x[pl.ds(plain + k * PIECE, PIECE), last], EDGE, 1)
+        lower = x[pl.ds(plain + packed + k * PIECE, PIECE), last]
+        rim_out[here] = jnp.where(iota((PIECE, LANES), 1) < EDGE, upper, lower).astype(BF16)
         forward.append(pltpu.make_async_remote_copy(
-            src_ref=rim_out.at[pieces[k]], dst_ref=rim_in.at[pieces[k]],
+            src_ref=rim_out.at[here], dst_ref=rim_in.at[here],
             send_sem=send_sem.at[k], recv_sem=recv_sem.at[k],
             device_id=right_id, device_id_type=MESH,
         ))
-        forward[k].start()
+        forward[-1].start()
     backward = pltpu.make_async_remote_copy(
         src_ref=edge_out, dst_ref=edge_in, send_sem=send_sem.at[PIECES], recv_sem=recv_sem.at[PIECES],
         device_id=left_id, device_id_type=MESH,
@@ -109,7 +118,9 @@
     rows_at = iota((LANES, LANES), 0)
     match_top = one_hot(rows_at == link_row)
     match_bottom = one_hot(rows_at - EDGE == link_row)
-    spot[...] = jnp.concatenate([links[...], links[...] + EDGE], axis=1)
+    nowhere = jnp.zeros((1, LANES - EDGE), jnp.int32)
+    spot[:1] = jnp.concatenate([links[...], nowhere], axis=1)
+    spot[1:] = jnp.concatenate([links[...] + EDGE, nowhere], axis=1)
 
     loads[0].wait()
     xb[:width, :LANES] = x[:, :LANES].astype(BF16)
@@ -117,6 +128,7 @@
         mm_nt(xb[:half, :LANES], match_top) + mm_nt(xb[half:width, :LANES], match_bottom)
     ).astype(BF16)
     loads[1].wait()
+    loads[2].wait()
     for t in range(1, tiles):
         xb[:width, lane_tile(t)] = x[:, lane_tile(t)].astype(BF16)
 
@@ -191,29 +203,33 @@
         backward.start()
 
     for copy in forward:
+        copy.wait_send()
+    backward.wait_send()
+
+    for copy in forward:
         copy.wait_recv()
     came[...] = rim_in[...]
-    for copy in forward:
-        copy.wait_send()
-    backward.wait_send()
-
-
-def finish(part, came, spot, dt, out, left, sem):
+    came_plain[...] = plain_in[...]
+
+
+def finish(part, came, came_plain, spot, dt, out, left, sem):
     rest = pltpu.make_async_copy(part.at[:, LANES:], out.at[:, LANES:], sem.at[0])
     rest.start()
-    half = came.shape[0]
-    width = 2 * half
-    found = jnp.take_along_axis(came[...].astype(F32), jnp.broadcast_to(spot[...], (half, LANES)), axis=1)
-    matched = jnp.concatenate([found, pltpu.roll(found, EDGE, 1)], axis=0)
-    matched = jnp.where(iota((width, LANES), 1) < EDGE, matched, 0.0)
-    rounded = matched.astype(BF16)
     copies = [rest]
-    rows = width // PIECES
-    for k in range(PIECES):
-        at = slice(k * rows, (k + 1) * rows)
-        left[at] = part[at, :LANES] + 0.5 * (matched[at] + mm(dt[at], rounded))
-        here = pl.ds(k * rows, rows)
-        copies.append(pltpu.make_async_copy(left.at[here], out.at[here, :LANES], sem.at[1 + k]))
+    packed = came.shape[0]
+    plain = came_plain.shape[0]
+
+    def pick(rows, k):
+        lanes = jnp.broadcast_to(spot[k:k + 1], rows.shape)
+        return jnp.where(iota(rows.shape, 1) < EDGE, jnp.take_along_axis(rows, lanes, axis=1), 0.0)
+
+    both = came[...].astype(F32)
+    matched = [pick(came_plain[...], 1), pick(both, 0), pick(both, 1)]
+    rounded = jnp.concatenate(matched, axis=0).astype(BF16)
+    for k, (start, rows) in enumerate(((0, plain), (plain, packed), (plain + packed, packed))):
+        at = pl.ds(start, rows)
+        left[at] = part[at, :LANES] + 0.5 * (matched[k] + mm(dt[at], rounded))
+        copies.append(pltpu.make_async_copy(left.at[at], out.at[at, :LANES], sem.at[1 + k]))
         copies[-1].start()
     for copy in copies:
         copy.wait()
@@ -225,18 +241,20 @@
     def per_device(state, cost, links, dyn_weight, rad_weight, cloud_weight):
         cols, width = state.shape
         half = width // 2
+        packed = PIECES * PIECE
         held = [state.T, cost.reshape(1, cols), links, dyn_weight, rad_weight, cloud_weight]
         held = [pltpu.with_memory_space_constraint(one, pltpu.HBM) for one in held]
         parts = pl.pallas_call(
             functools.partial(kernel, n_grp, n_peer),
             out_shape=[
                 jax.ShapeDtypeStruct((width, cols), F32),
-                jax.ShapeDtypeStruct((half, LANES), BF16),
-                jax.ShapeDtypeStruct((1, LANES), jnp.int32),
+                jax.ShapeDtypeStruct((packed, LANES), BF16),
+                jax.ShapeDtypeStruct((width - 2 * packed, LANES), F32),
+                jax.ShapeDtypeStruct((2, LANES), jnp.int32),
                 jax.ShapeDtypeStruct((width, width), BF16),
             ],
             in_specs=[pl.BlockSpec(memory_space=pltpu.HBM)] * 6,
-            out_specs=[pl.BlockSpec(memory_space=pltpu.VMEM)] * 4,
+            out_specs=[pl.BlockSpec(memory_space=pltpu.VMEM)] * 5,
             scratch_shapes=[
                 pltpu.VMEM((width, cols), F32),
                 pltpu.VMEM((1, cols), jnp.int32),
@@ -251,14 +269,15 @@
                 pltpu.VMEM((width, SLOTS), F32),
                 pltpu.VMEM((width, SLOTS), F32),
                 pltpu.VMEM((width, SLOTS), F32),
-                pltpu.VMEM((half, LANES), BF16),
-                pltpu.VMEM((half, LANES), BF16),
+                pltpu.VMEM((packed, LANES), BF16),
+                pltpu.VMEM((packed, LANES), BF16),
+                pltpu.VMEM((width - 2 * packed, LANES), F32),
                 pltpu.VMEM((half, LANES), BF16),
                 pltpu.VMEM((half, LANES), BF16),
                 pltpu.SemaphoreType.DMA((2 * PIECES,)),
-                pltpu.SemaphoreType.DMA((7,)),
-                pltpu.SemaphoreType.DMA((PIECES + 1,)),
-                pltpu.SemaphoreType.DMA((PIECES + 1,)),
+                pltpu.SemaphoreType.DMA((8,)),
+                pltpu.SemaphoreType.DMA((PIECES + 2,)),
+                pltpu.SemaphoreType.DMA((PIECES + 2,)),
                 pltpu.SemaphoreType.REGULAR,
             ],
             compiler_params=pltpu.CompilerParams(
@@ -268,9 +287,9 @@
         flipped = pl.pallas_call(
             finish,
             out_shape=jax.ShapeDtypeStruct((width, cols), F32),
-            in_specs=[pl.BlockSpec(memory_space=pltpu.VMEM)] * 4,
+            in_specs=[pl.BlockSpec(memory_space=pltpu.VMEM)] * 5,
             out_specs=pl.BlockSpec(memory_space=pltpu.HBM),
-            scratch_shapes=[pltpu.VMEM((width, LANES), F32), pltpu.SemaphoreType.DMA((1 + PIECES,))],
+            scratch_shapes=[pltpu.VMEM((width, LANES), F32), pltpu.SemaphoreType.DMA((4,))],
             compiler_params=pltpu.CompilerParams(vmem_limit_bytes=8 * 2**20),
         )(*[pltpu.with_memory_space_constraint(one, pltpu.VMEM) for one in parts])
         return flipped.T

time: 19.6 us -> 19.4 us (0.990)
  Pallas kernels: 19.5 us -> 19.3 us
where the time goes in v4:
time: 19.4 us; the launch traced here: 19.3 us
  Pallas kernels  19.3 us (99%)
    pallas_call x1, Pallas kernels, per_device(): pl.pallas_call(functools.partial(kernel, n_grp, n_peer), out_shape=[jax.S...  18.3 us
    pallas_call x1, Pallas kernels, per_device(): pl.pallas_call(finish, out_shape=jax.ShapeDtypeStruct((width, cols), F32)...  0.95 us

profile of v4, /device:TPU:56, one launch (start us, length us, event | category | flops | bytes accessed | tf_op | source)
XLA Modules:
  0.0 19.3 jit_solution(3414082089771010467)
XLA Ops:
  0.0 18.3 %shard_map.64 = (f32[288,512]{1,0:T(8,128)S(1)}, bf16[96,128]{1,0:T(8,128)(2,1)S(1)}, f32[96,128]{1,0:T(8,128)S(1)}, s32[2,128]{1,0:T(2,128)S(1)}, bf16[288,288]{1,0:T(8,128)(2,1)S(1)}) custom-call(f32[288,512]{1,0:T(8,128)} %bitcast.3, s32[1,512]{1,0:T(1,128)} %bitcast.4, s32[1,64]{1,0:T(1,128)} %links_hbm.1, bf16[288,288]{1,0:T(8,128)(2,1)} %wd_hbm.1, ...), custom_call_target="tpu_custom_call" | custom-call | tf_op jit(solution)/shard_map/pallas_call | solution.py:247
  18.3 0.9 %shard_map.65 = f32[288,512]{1,0:T(8,128)} custom-call(f32[288,512]{1,0:T(8,128)S(1)} %get-tuple-element.10.part, bf16[96,128]{1,0:T(8,128)(2,1)S(1)} %get-tuple-element.11.came, f32[96,128]{1,0:T(8,128)S(1)} %get-tuple-element.12.came_plain, s32[2,128]{1,0:T(2,128)S(1)} %get-tuple-element.13.spot, bf16[288,288]{1,0:T(8,128)(2,1)S(1)} %get-tuple-element.14.dt), custom_call_target="tpu_custom_call" | custom-call | tf_op jit(solution)/shard_map/pallas_call | solution.py:287

commit v5 on v4

--- a/solution.py
+++ b/solution.py
@@ -39,9 +39,9 @@
 def kernel(
     n_grp, n_peer,
     x_hbm, cost_hbm, links_hbm, wd_hbm, wr_hbm, wc_hbm,
-    out, came, came_plain, spot, dt,
+    out, came, spot, dt_rest,
     x, cost, links, wd, wr, wc,
-    xb, wct, wdr, pt, first, now, mask, rim_out, rim_in, plain_in, edge_out, edge_in,
+    xb, wct, wdr, dt, pt, first, now, mask, rim_out, rim_in, plain_in, edge_out, edge_in,
     rim_sem, load_sem, send_sem, recv_sem, ready_sem,
 ):
     width, cols = x.shape
@@ -178,6 +178,8 @@
     two = mm(wdt, wdt)
     three = mm(wdt, two.astype(BF16))
     dt[...] = (0.6 * wdt.astype(F32) + 0.12 * two + 0.008 * three).astype(BF16)
+    tail = (width, width - plain)
+    dt_rest[...] = mm(dt[...], one_hot(iota(tail, 0) - plain == iota(tail, 1))).astype(BF16)
 
     for t in range(cols // WIDE):
         at = pl.ds(t * WIDE, WIDE)
@@ -206,29 +208,35 @@
         copy.wait_send()
     backward.wait_send()
 
-    for copy in forward:
+    forward[0].wait_recv()
+    head = mm(plain_in[...].astype(BF16), match_bottom)
+    out[:plain, :LANES] = out[:plain, :LANES] + 0.5 * head
+    out[:, :LANES] = out[:, :LANES] + 0.5 * mm(dt[:, :plain], head.astype(BF16))
+    for copy in forward[1:]:
         copy.wait_recv()
     came[...] = rim_in[...]
-    came_plain[...] = plain_in[...]
-
-
-def finish(part, came, came_plain, spot, dt, out, left, sem):
+
+
+def finish(part, came, spot, dt_rest, out, left, sem):
     rest = pltpu.make_async_copy(part.at[:, LANES:], out.at[:, LANES:], sem.at[0])
     rest.start()
     copies = [rest]
     packed = came.shape[0]
-    plain = came_plain.shape[0]
-
-    def pick(rows, k):
-        lanes = jnp.broadcast_to(spot[k:k + 1], rows.shape)
-        return jnp.where(iota(rows.shape, 1) < EDGE, jnp.take_along_axis(rows, lanes, axis=1), 0.0)
-
+    plain = part.shape[0] - 2 * packed
     both = came[...].astype(F32)
-    matched = [pick(came_plain[...], 1), pick(both, 0), pick(both, 1)]
+
+    def pick(k):
+        lanes = jnp.broadcast_to(spot[k:k + 1], both.shape)
+        return jnp.where(iota(both.shape, 1) < EDGE, jnp.take_along_axis(both, lanes, axis=1), 0.0)
+
+    matched = [pick(0), pick(1)]
     rounded = jnp.concatenate(matched, axis=0).astype(BF16)
     for k, (start, rows) in enumerate(((0, plain), (plain, packed), (plain + packed, packed))):
         at = pl.ds(start, rows)
-        left[at] = part[at, :LANES] + 0.5 * (matched[k] + mm(dt[at], rounded))
+        turned = mm(dt_rest[at], rounded)
+        if k > 0:
+            turned = turned + matched[k - 1]
+        left[at] = part[at, :LANES] + 0.5 * turned
         copies.append(pltpu.make_async_copy(left.at[at], out.at[at, :LANES], sem.at[1 + k]))
         copies[-1].start()
     for copy in copies:
@@ -249,12 +257,11 @@
             out_shape=[
                 jax.ShapeDtypeStruct((width, cols), F32),
                 jax.ShapeDtypeStruct((packed, LANES), BF16),
-                jax.ShapeDtypeStruct((width - 2 * packed, LANES), F32),
                 jax.ShapeDtypeStruct((2, LANES), jnp.int32),
-                jax.ShapeDtypeStruct((width, width), BF16),
+                jax.ShapeDtypeStruct((width, 2 * packed), BF16),
             ],
             in_specs=[pl.BlockSpec(memory_space=pltpu.HBM)] * 6,
-            out_specs=[pl.BlockSpec(memory_space=pltpu.VMEM)] * 5,
+            out_specs=[pl.BlockSpec(memory_space=pltpu.VMEM)] * 4,
             scratch_shapes=[
                 pltpu.VMEM((width, cols), F32),
                 pltpu.VMEM((1, cols), jnp.int32),
@@ -265,6 +272,7 @@
                 pltpu.VMEM((width + 16, cols), BF16),
                 pltpu.VMEM((width, width), BF16),
                 pltpu.VMEM((2 * width, width), BF16),
+                pltpu.VMEM((width, width), BF16),
                 pltpu.VMEM((SLOTS, cols), BF16),
                 pltpu.VMEM((width, SLOTS), F32),
                 pltpu.VMEM((width, SLOTS), F32),
@@ -287,7 +295,7 @@
         flipped = pl.pallas_call(
             finish,
             out_shape=jax.ShapeDtypeStruct((width, cols), F32),
-            in_specs=[pl.BlockSpec(memory_space=pltpu.VMEM)] * 5,
+            in_specs=[pl.BlockSpec(memory_space=pltpu.VMEM)] * 4,
             out_specs=pl.BlockSpec(memory_space=pltpu.HBM),
             scratch_shapes=[pltpu.VMEM((width, LANES), F32), pltpu.SemaphoreType.DMA((4,))],
             compiler_params=pltpu.CompilerParams(vmem_limit_bytes=8 * 2**20),

time: 19.4 us -> 19.4 us (level)
  no operation moved by 1% of the time
where the time goes in v5:
time: 19.4 us; the launch traced here: 19.3 us
  Pallas kernels  19.3 us (99%)
    pallas_call x1, Pallas kernels, per_device(): pl.pallas_call(functools.partial(kernel, n_grp, n_peer), out_shape=[jax.S...  18.3 us
    pallas_call x1, Pallas kernels, per_device(): pl.pallas_call(finish, out_shape=jax.ShapeDtypeStruct((width, cols), F32)...  0.94 us

profile of v5, /device:TPU:56, one launch (start us, length us, event | category | flops | bytes accessed | tf_op | source)
XLA Modules:
  0.0 19.3 jit_solution(5977155027965586834)
XLA Ops:
  0.0 18.3 %shard_map.64 = (f32[288,512]{1,0:T(8,128)S(1)}, bf16[96,128]{1,0:T(8,128)(2,1)S(1)}, s32[2,128]{1,0:T(2,128)S(1)}, bf16[288,192]{1,0:T(8,128)(2,1)S(1)}) custom-call(f32[288,512]{1,0:T(8,128)} %bitcast.3, s32[1,512]{1,0:T(1,128)} %bitcast.4, s32[1,64]{1,0:T(1,128)} %links_hbm.1, bf16[288,288]{1,0:T(8,128)(2,1)} %wd_hbm.1, bf16[288,288]{1,0:T(8,128)(2,1)} %wr_hbm.1, ...), custom_call_target="tpu_custom_call" | custom-call | tf_op jit(solution)/shard_map/pallas_call | solution.py:255
  18.3 0.9 %shard_map.65 = f32[288,512]{1,0:T(8,128)} custom-call(f32[288,512]{1,0:T(8,128)S(1)} %get-tuple-element.9.part, bf16[96,128]{1,0:T(8,128)(2,1)S(1)} %get-tuple-element.10.came, s32[2,128]{1,0:T(2,128)S(1)} %get-tuple-element.11.spot, bf16[288,192]{1,0:T(8,128)(2,1)S(1)} %get-tuple-element.12.dt_rest), custom_call_target="tpu_custom_call" | custom-call | tf_op jit(solution)/shard_map/pallas_call | solution.py:295
